TPU v7x, 32 devices: a whole 2x2x4 slice. The times are simulated.
32 devices in a mesh: group: 2 (over y), row: 4 (over z), col: 4 (over x, core).
Axes of the slice: x: 2, y: 2, z: 4, core: 2. Of those that a mesh axis runs over, the one named last changes fastest.
Arguments:
- pair_repr: bfloat16 [256, 128, 128], P(('group', 'row'), 'col'), parts along dimension 0, may hold values from -6 to 6
- chain_ids: int32 [256], P('group'), parts along dimension 0, may hold values from 0 to 7, never falling along the last dimension, each value on 1 to 32 neighbouring positions
- valid_counts: int32 [16], P('group'), parts along dimension 0, may hold values from 8 to 32
- norm_gain: float32 [128], replicated, may hold values from 0.25 to 1.75
- norm_bias: float32 [128], replicated, may hold values from -3 to 3
- input_weights: bfloat16 [128, 384], replicated, may hold values from -0.5 to 0.5
- final_gain: float32 [64], replicated, may hold values from 0.25 to 1.75
- final_bias: float32 [64], replicated, may hold values from -3 to 3
- output_weight: bfloat16 [64, 128], replicated, may hold values from -0.75 to 0.75
- transition_in: bfloat16 [128, 1024], replicated, may hold values from -0.5 to 0.5
- transition_out: bfloat16 [512, 128], replicated, may hold values from -0.25 to 0.25
Outputs:
- update: bfloat16 [256, 128, 128], P(('group', 'row', 'col')), parts along dimension 0
There are 2 independent parts, one for each index of `group`. A program takes and returns all parts, laid end to end along the dimension named above; an argument that names none is the same for every part. Nothing has to cross between parts.
Inputs may be any that keep to these rules, and one draw needn't show every extreme that they name: chain_ids never falls; each chain holds 1 to 32 tokens and one holds exactly 32.
All inputs are finite; a program needn't handle non-finite values.
Results may differ from a plain program's by a relative error of at most 0.0063.
Values may be sent and summed in bfloat16 or wider, within the bound.
A program may use at most 192 MiB of HBM per device.

v0:
```python
import jax
import jax.numpy as jnp
from jax import lax
from jax.sharding import PartitionSpec as P


def token_valid_of(chain_ids, valid_counts):
    token_count = chain_ids.shape[0]
    labels = jnp.arange(valid_counts.shape[0], dtype=jnp.int32)
    before = (chain_ids[:, None] < labels[None, :]).astype(jnp.int32)
    starts = jnp.sum(before, axis=0)
    member = (chain_ids[:, None] == labels[None, :]).astype(jnp.int32)
    first_index = jnp.sum(member * starts[None, :], axis=1)
    limits = jnp.sum(member * valid_counts[None, :], axis=1)
    position = jnp.arange(token_count, dtype=jnp.int32) - first_index
    return (position < limits).astype(jnp.float32)


def layer_norm(values, gain, bias):
    average = jnp.mean(values, axis=-1, keepdims=True)
    centered = values - average
    spread = jnp.mean(centered * centered, axis=-1, keepdims=True)
    return centered * lax.rsqrt(spread + 1e-05) * gain + bias


def local(
    pair_repr,
    chain_ids,
    valid_counts,
    norm_gain,
    norm_bias,
    input_weights,
    final_gain,
    final_bias,
    output_weight,
    transition_in,
    transition_out,
):
    row_count, col_count, channels = pair_repr.shape
    hidden = output_weight.shape[0]
    trans_width = transition_out.shape[0]
    token_valid = token_valid_of(chain_ids, valid_counts)
    row_start = lax.axis_index("row") * row_count
    col_start = lax.axis_index("col") * col_count
    valid_rows = lax.dynamic_slice_in_dim(token_valid, row_start, row_count)
    valid_cols = lax.dynamic_slice_in_dim(token_valid, col_start, col_count)
    pair_valid = valid_rows[:, None] * valid_cols[None, :]
    normed = layer_norm(pair_repr.astype(jnp.float32), norm_gain, norm_bias).astype(jnp.bfloat16)
    normed_flat = normed.reshape(row_count * col_count, channels)
    projected = jnp.dot(normed_flat, input_weights, preferred_element_type=jnp.float32)
    projected = projected.reshape(row_count, col_count, 4 * hidden + channels)
    left_side = (
        jax.nn.sigmoid(projected[..., hidden : 2 * hidden])
        * projected[..., :hidden]
        * pair_valid[..., None]
    ).astype(jnp.bfloat16)
    right_side = (
        jax.nn.sigmoid(projected[..., 3 * hidden : 4 * hidden])
        * projected[..., 2 * hidden : 3 * hidden]
        * pair_valid[..., None]
    ).astype(jnp.bfloat16)
    gate_value = jax.nn.sigmoid(projected[..., 4 * hidden :])
    both_parts = jnp.dot(normed_flat, transition_in, preferred_element_type=jnp.float32)
    hidden_act = (jax.nn.silu(both_parts[:, :trans_width]) * both_parts[:, trans_width:]).astype(
        jnp.bfloat16
    )
    transition = jnp.dot(hidden_act, transition_out, preferred_element_type=jnp.float32).reshape(
        row_count, col_count, channels
    )
    partials = jnp.einsum(
        "ikc,jkc->ijc",
        left_side,
        lax.all_gather(right_side, "row", axis=0, tiled=True),
        preferred_element_type=jnp.float32,
    )
    mixed_sum = lax.psum_scatter(partials, "col", scatter_dimension=1, tiled=True)
    mixed_normed = layer_norm(mixed_sum, final_gain, final_bias).astype(jnp.bfloat16)
    outgoing = jnp.dot(
        mixed_normed.reshape(row_count * col_count, hidden),
        output_weight,
        preferred_element_type=jnp.float32,
    )
    update_tile = (
        gate_value * outgoing.reshape(row_count, col_count, channels) + transition
    ).astype(jnp.bfloat16)
    return lax.all_to_all(update_tile, "col", split_axis=0, concat_axis=1, tiled=True)


def solution(mesh):
    in_specs = (
        P(("group", "row"), "col", None),
        P("group"),
        P("group"),
        P(),
        P(),
        P(),
        P(),
        P(),
        P(),
        P(),
        P(),
    )
    out_specs = P(("group", "row", "col"), None, None)
    return jax.shard_map(local, mesh=mesh, in_specs=in_specs, out_specs=out_specs, check_vma=False)
```

profile of v0, /device:TPU:0, one launch (start us, length us, event | category | flops | bytes accessed | tf_op | source)
XLA Modules:
  0.0 101.2 jit_solution(9565993777036422716)
XLA Ops:
  6.6 1.2 %convert_reduce_fusion = f32[32,32]{1,0:T(8,128)S(1)} fusion(bf16[32,32,128]{2,1,0:T(8,128)(2,1)} %param.11), kind=kLoop, calls=%fused_computation.8 | loop fusion | flops 261120 | bytes 266240 | tf_op jit(solution)/shard_map/reduce_sum | solution.py:20
  7.8 1.3 %fusion.7 = f32[32,32]{1,0:T(8,128)S(1)} fusion(bf16[32,32,128]{2,1,0:T(8,128)(2,1)} %param.11, f32[32,32]{1,0:T(8,128)S(1)} %broadcast_multiply_fusion.2), kind=kLoop, calls=%fused_computation.11 | loop fusion | flops 523264 | bytes 270336 | tf_op jit(solution)/shard_map/reduce_sum | solution.py:22
  9.1 0.8 convert_reduce_fusion.1
  9.9 1.3 %fusion.10 = bf16[32,32,128]{2,1,0:T(8,128)(2,1)S(1)} fusion(bf16[32,32,128]{2,1,0:T(8,128)(2,1)} %param.11, f32[128]{0:T(128)} %param.15, f32[128]{0:T(128)} %param.14, f32[32,32]{1,0:T(8,128)S(1)} %add_rsqrt_fusion.1, f32[32,32]{1,0:T(8,128)S(1)} %broadcast_multiply_fusion.2), kind=kLoop, calls=%fused_computation.14 | loop fusion | flops 786432 | bytes 533504 | tf_op jit(solution)/shard_map/convert_element_type | solution.py:48
  11.2 1.2 %fusion.25 = f32[32,32,384]{2,1,0:T(8,128)S(1)} fusion(bf16[32,32,128]{2,1,0:T(8,128)(2,1)S(1)} %fusion.10, bf16[128,384]{1,0:T(8,128)(2,1)} %param.16), kind=kOutput, calls=%fused_computation.36 | convolution fusion | flops 100663296 | bytes 1933312 | tf_op jit(solution)/shard_map/dot_general | solution.py:50
  12.5 0.1 select_reduce_fusion.1
  12.6 0.1 fusion.29
  12.7 0.5 fusion.12
  13.2 24.2 %all_gather.3 = bf16[128,32,64]{2,1,0:T(8,128)(2,1)S(1)} all-gather(bf16[32,32,64]{2,1,0:T(8,128)(2,1)S(1)} %get-tuple-element.8), channel_id=1, replica_groups=mesh['group'=2,'row'=4,'col'=4] {'row'}, dimensions={0}, use_global_device_ids=true | all-gather | bytes 655360 | tf_op jit(solution)/shard_map/all_gather | solution.py:73
  37.4 3.9 %copy.39 = bf16[128,32,64]{1,0,2:T(8,128)(2,1)} copy(bf16[128,32,64]{2,1,0:T(8,128)(2,1)S(1)} %all_gather.3) | data formatting | bytes 1048576 | tf_op jit(solution)/shard_map/all_gather | solution.py:73
  41.3 1.5 %copy.40 = bf16[32,32,64]{1,0,2:T(8,128)(2,1)} copy(bf16[32,32,64]{2,1,0:T(8,128)(2,1)S(1)} %get-tuple-element.7) | data formatting | bytes 262144 | tf_op jit(solution)/shard_map/convert_element_type | solution.py:56
  42.8 2.9 %convolution_bitcast_fusion = f32[32,128,64]{1,0,2:T(8,128)S(1)} fusion(bf16[128,32,64]{1,0,2:T(8,128)(2,1)} %copy.39, bf16[32,32,64]{1,0,2:T(8,128)(2,1)} %copy.40), kind=kOutput, calls=%fused_computation.2 | convolution fusion | flops 16777216 | bytes 1703936 | tf_op jit(solution)/shard_map/ikc,jkc->ijc/dot_general | solution.py:70
  45.7 3.0 %copy.41 = f32[32,128,64]{2,0,1:T(8,128)} copy(f32[32,128,64]{1,0,2:T(8,128)S(1)} %convolution_bitcast_fusion) | data formatting | bytes 2097152 | tf_op jit(solution)/shard_map/ikc,jkc->ijc/transpose | solution.py:70
  48.7 0.7 fusion.30
  49.4 0.2 copy-done.5
  49.6 0.7 fusion.3
  50.3 30.2 %reduce-scatter.2.cloned.1.call-done = f32[32,32,64]{2,0,1:T(8,128)} async-done(((f32[32,128,64]{2,0,1:T(8,128)}), f32[32,32,64]{2,0,1:T(8,128)}) %reduce-scatter.2.cloned.1.call-update) | async-done | bytes 262160 | tf_op jit(solution)/shard_map/reduce_scatter | solution.py:76
  80.5 1.2 %reduce_sum.68 = f32[32,32]{0,1:T(8,128)S(1)} reduce(f32[32,32,64]{2,0,1:T(8,128)} %reduce-scatter.2.cloned.1.call-done, f32[]{:T(128)} %constant.11.clone.1), dimensions={2}, to_apply=%region_6.7 | reduce | flops 64512 | bytes 266244 | tf_op jit(solution)/shard_map/reduce_sum | solution.py:20
  81.8 0.1 copy.43
  81.9 1.4 %multiply_reduce_fusion = f32[32,32]{0,1:T(8,128)S(1)} fusion(f32[32,32,64]{2,0,1:T(8,128)} %reduce-scatter.2.cloned.1.call-done, f32[32,32]{0,1:T(8,128)S(1)} %copy.43), kind=kLoop, calls=%fused_computation.34 | loop fusion | flops 195584 | bytes 270336 | tf_op jit(solution)/shard_map/reduce_sum | solution.py:22
  83.5 1.4 %add_convert_fusion = bf16[32,32,64]{2,0,1:T(8,128)(2,1)S(1)} fusion(f32[32,32,64]{2,0,1:T(8,128)} %reduce-scatter.2.cloned.1.call-done, f32[64]{0:T(128)S(1)} %copy-done.1, f32[64]{0:T(128)S(1)} %copy-done.2, f32[32,32]{0,1:T(8,128)S(1)} %copy.45, f32[32,32]{0,1:T(8,128)S(1)} %copy.43), kind=kLoop, calls=%fused_computation.33 | loop fusion | flops 327680 | bytes 401920 | tf_op jit(solution)/shard_map/convert_element_type | solution.py:77
  84.9 0.3 fusion.2
  85.2 8.4 %all_to_all.18 = bf16[32,32,128]{2,1,0:T(8,128)(2,1)S(1)} all-to-all(bf16[32,32,128]{2,1,0:T(8,128)(2,1)S(1)} %fusion.2), channel_id=1, replica_groups=mesh['group'=2,'row'=4,'col'=4] {'col'}, dimensions={0} | all-to-all | bytes 524288 | tf_op jit(solution)/shard_map/all_to_all | solution.py:86
  93.6 0.7 copy.47
  (24 shorter events, 0.4 us)
Async XLA Ops:
  6.5 42.1 %copy-start = (bf16[128,1024]{1,0:T(8,128)(2,1)S(1)}, bf16[128,1024]{1,0:T(8,128)(2,1)}, u32[]{:S(2)}) copy-start(bf16[128,1024]{1,0:T(8,128)(2,1)} %param.20) | copy-start | bytes 786436
  6.5 5.9 %copy-start.3 = (s32[128]{0:T(128)S(1)}, s32[128]{0:T(128)}, u32[]{:S(2)}) copy-start(s32[128]{0:T(128)} %param.12) | copy-start | bytes 1540
  6.5 5.9 %copy-start.4 = (s32[8]{0:T(128)S(1)}, s32[8]{0:T(128)}, u32[]{:S(2)}) copy-start(s32[8]{0:T(128)} %param.13) | copy-start | bytes 100
  6.5 73.9 %reduce-scatter.2.cloned.1.call-start = ((), (), s32[]{:S(2)}) async-start(), calls=%async_computation.2 | async-start | bytes 2621440 | tf_op jit(solution)/shard_map/reduce_scatter | solution.py:76
  48.7 0.9 copy-start.5
  49.6 33.9 %copy-start.1 = (f32[64]{0:T(128)S(1)}, f32[64]{0:T(128)}, u32[]{:S(2)}) copy-start(f32[64]{0:T(128)} %param.18) | copy-start | bytes 772
  49.6 33.9 %copy-start.2 = (f32[64]{0:T(128)S(1)}, f32[64]{0:T(128)}, u32[]{:S(2)}) copy-start(f32[64]{0:T(128)} %param.17) | copy-start | bytes 772
  50.3 34.6 %copy-start.6 = (bf16[64,128]{1,0:T(8,128)(2,1)S(1)}, bf16[64,128]{1,0:T(8,128)(2,1)}, u32[]{:S(2)}) copy-start(bf16[64,128]{1,0:T(8,128)(2,1)} %param.19) | copy-start | bytes 49156
Sparse Core Ops, SparseCore 0:
  48.8 31.6 reduce-scatter.1
where the time goes:
time: 102 us; the launch traced here: 101 us
  blocking collectives  32.6 us (32%)
  waiting for transfers between devices  30.2 us (30%)
  between operations  13.6 us (13%)
  local copies, waits for them, and re-layouts  9.73 us (10%)
  other arithmetic  9.34 us (9%)
  matrix products  5.73 us (6%)
    reduce_scatter x1, waiting for transfers between devices, local(): lax.psum_scatter(partials, 'col', scatter_dimension=1, tiled=True)  30.2 us
    all_gather x1, blocking collectives, local(): lax.all_gather(right_side, 'row', axis=0, tiled=True)  24.2 us
    all_to_all x1, blocking collectives, local(): lax.all_to_all(update_tile, 'col', split_axis=0, concat_axis=1, tiled=True)  8.42 us
    all_gather x1, local copies, waits for them, and re-layouts, local(): lax.all_gather(right_side, 'row', axis=0, tiled=True)  3.92 us
    transpose x1, local copies, waits for them, and re-layouts, local(): jnp.einsum('ikc,jkc->ijc', left_side, lax.all_gather(right_side, 'row', a...  2.98 us
    dot_general x1, matrix products, local(): jnp.einsum('ikc,jkc->ijc', left_side, lax.all_gather(right_side, 'row', a...  2.85 us
    reduce_sum x2, other arithmetic, layer_norm(): spread = jnp.mean(centered * centered, axis=-1, keepdims=True)  2.75 us
    reduce_sum x2, other arithmetic, layer_norm(): average = jnp.mean(values, axis=-1, keepdims=True)  2.45 us
  transfers between devices with their start and end apart: 1, of which 1 were waited for; matrix products, arithmetic and copies ran while one was open for 1% of the time, Pallas kernels for 0%

commit v1 on v0

--- a/solution.py
+++ b/solution.py
@@ -1,7 +1,302 @@
+import functools
+
 import jax
 import jax.numpy as jnp
 from jax import lax
+from jax.experimental import pallas as pl
+from jax.experimental.pallas import tpu as pltpu
 from jax.sharding import PartitionSpec as P
+
+MESH = pl.DeviceIdType.MESH
+F32, BF16 = jnp.float32, jnp.bfloat16
+
+
+def sigmoid(v):
+    return 0.5 * jnp.tanh(0.5 * v) + 0.5
+
+
+def column_of(row):
+    n = row.shape[1]
+    spot = lax.broadcasted_iota(jnp.int32, (n, n), 0) == lax.broadcasted_iota(jnp.int32, (n, n), 1)
+    return jnp.sum(jnp.where(spot, row, 0.0), axis=1, keepdims=True)
+
+
+def kernel(
+    rows_n,
+    cols_n,
+    pair_ref,
+    ids_ref,
+    counts_ref,
+    gain_ref,
+    bias_ref,
+    in_hbm,
+    fgain_ref,
+    fbias_ref,
+    out_hbm,
+    tin_hbm,
+    tout_hbm,
+    update_ref,
+    x_ref,
+    win_ref,
+    wout_ref,
+    tin_ref,
+    tout_ref,
+    normed_ref,
+    lr_ref,
+    rx_ref,
+    tx_ref,
+    mx_ref,
+    gate_ref,
+    trans_ref,
+    local_sem,
+    in_send,
+    in_recv,
+    a_send,
+    a_recv,
+    b_send,
+    b_recv,
+):
+    peers = rows_n * cols_n
+    own, tokens, channels = x_ref.shape
+    width = pair_ref.shape[1]
+    hidden = wout_ref.shape[0]
+    trans = tout_ref.shape[0]
+    share = hidden // peers
+    row, col = lax.axis_index("row"), lax.axis_index("col")
+    me = row * cols_n + col
+
+    def at(offset):
+        peer = lax.rem(me + offset, peers)
+        return {"row": lax.div(peer, cols_n), "col": lax.rem(peer, cols_n)}, peer
+
+    barrier = pltpu.get_barrier_semaphore()
+    for o in range(1, peers):
+        pl.semaphore_signal(barrier, inc=1, device_id=at(o)[0], device_id_type=MESH)
+    locals_ = [
+        pltpu.make_async_copy(
+            pair_ref.at[pl.ds(col * own, own)],
+            x_ref.at[:, pl.ds(col * width, width), :],
+            local_sem.at[0],
+        )
+    ]
+    for n, (a, b) in enumerate(
+        ((in_hbm, win_ref), (out_hbm, wout_ref), (tin_hbm, tin_ref), (tout_hbm, tout_ref))
+    ):
+        locals_.append(pltpu.make_async_copy(a, b, local_sem.at[n + 1]))
+    for c in locals_:
+        c.start()
+    pl.semaphore_wait(barrier, peers - 1)
+
+    copies = []
+    for o in range(1, cols_n):
+        to = lax.rem(col + o, cols_n)
+        copies.append(
+            pltpu.make_async_remote_copy(
+                src_ref=pair_ref.at[pl.ds(to * own, own)],
+                dst_ref=x_ref.at[:, pl.ds(col * width, width), :],
+                send_sem=in_send.at[o],
+                recv_sem=in_recv.at[o],
+                device_id={"row": row, "col": to},
+                device_id_type=MESH,
+            )
+        )
+    for c in copies:
+        c.start()
+
+    ids = ids_ref[...]
+    first = jnp.zeros(ids.shape, F32)
+    limit = jnp.zeros(ids.shape, jnp.int32)
+    for label in range(counts_ref.shape[0]):
+        start = jnp.sum(jnp.where(ids < label, 1.0, 0.0), axis=1, keepdims=True)
+        first = jnp.where(ids == label, start, first)
+        limit = jnp.where(ids == label, counts_ref[label], limit)
+    spot = lax.broadcasted_iota(jnp.int32, ids.shape, 1).astype(F32)
+    valid = jnp.where(spot - first < limit.astype(F32), 1.0, 0.0)
+    wide = (own, tokens)
+    mine = lax.broadcasted_iota(jnp.int32, wide, 1) == (
+        me * own + lax.broadcasted_iota(jnp.int32, wide, 0)
+    )
+    valid_rows = jnp.sum(jnp.where(mine, valid, 0.0), axis=1, keepdims=True)
+    pair_valid = valid_rows * valid
+    fgain, fbias = column_of(fgain_ref[...]), column_of(fbias_ref[...])
+    for c in locals_:
+        c.wait()
+    in_t = win_ref[:, : 4 * hidden].astype(F32).T.astype(BF16)
+    for c in copies:
+        c.wait()
+
+    x = x_ref[...].reshape(own * tokens, channels).astype(F32)
+    average = jnp.mean(x, axis=-1, keepdims=True)
+    centered = x - average
+    spread = jnp.mean(centered * centered, axis=-1, keepdims=True)
+    normed = (centered * lax.rsqrt(spread + 1e-05) * gain_ref[...] + bias_ref[...]).astype(BF16)
+    normed_ref[...] = normed
+
+    projected = lax.dot_general(in_t, normed, (((1,), (1,)), ((), ())), preferred_element_type=F32)
+    left = sigmoid(projected[hidden : 2 * hidden]) * projected[:hidden]
+    right = sigmoid(projected[3 * hidden :]) * projected[2 * hidden : 3 * hidden]
+
+    def by_channel(v):
+        parts = [v[:, i * tokens : (i + 1) * tokens] for i in range(own)]
+        return jnp.transpose(jnp.stack(parts, axis=0), (1, 0, 2)) * pair_valid
+
+    both = jnp.concatenate([by_channel(left), by_channel(right)], axis=1)
+    lr_ref[...] = both.astype(BF16)
+
+    sends = []
+    for o in range(1, peers):
+        device, peer = at(o)
+        sends.append(
+            pltpu.make_async_remote_copy(
+                src_ref=lr_ref.at[pl.ds(peer * share, share)],
+                dst_ref=rx_ref.at[me],
+                send_sem=a_send.at[o],
+                recv_sem=a_recv.at[o],
+                device_id=device,
+                device_id_type=MESH,
+            )
+        )
+    for c in sends:
+        c.start()
+    rx_ref[me] = lr_ref[pl.ds(me * share, share)]
+
+    gate_ref[...] = sigmoid(
+        jnp.dot(normed_ref[...], win_ref[:, 4 * hidden :], preferred_element_type=F32)
+    )
+    step = 128
+
+    @pl.loop(0, own * tokens // step)
+    def _(n):
+        where = pl.ds(pl.multiple_of(n * step, step), step)
+        part = jnp.dot(normed_ref[where], tin_ref[...], preferred_element_type=F32)
+        ta, tb = part[:, :trans], part[:, trans:]
+        act = (ta * sigmoid(ta) * tb).astype(BF16)
+        trans_ref[where] = jnp.dot(act, tout_ref[...], preferred_element_type=F32)
+
+    for c in sends:
+        c.wait()
+    mixed = []
+    for h in range(share):
+        block = rx_ref[:, h].astype(F32)
+        lh = block[:, :own].reshape(tokens, tokens).astype(BF16)
+        rh = block[:, own:].reshape(tokens, tokens).astype(BF16)
+        m = lax.dot_general(lh, rh, (((1,), (1,)), ((), ())), preferred_element_type=F32)
+        mixed.append(m.reshape(peers, own, tokens))
+    for n in range(share // 2):
+        tx_ref[:, n] = jnp.concatenate(mixed[2 * n : 2 * n + 2], axis=1).astype(BF16)
+    backs = []
+    for o in range(1, peers):
+        device, peer = at(o)
+        backs.append(
+            pltpu.make_async_remote_copy(
+                src_ref=tx_ref.at[peer],
+                dst_ref=mx_ref.at[me],
+                send_sem=b_send.at[o],
+                recv_sem=b_recv.at[o],
+                device_id=device,
+                device_id_type=MESH,
+            )
+        )
+    for c in backs:
+        c.start()
+    mx_ref[me] = tx_ref[me]
+    for c in backs:
+        c.wait()
+
+    m = mx_ref[...].astype(F32).reshape(hidden, own, tokens)
+    average = jnp.mean(m, axis=0, keepdims=True)
+    centered = m - average
+    spread = jnp.mean(centered * centered, axis=0, keepdims=True)
+    scaled = jnp.transpose(centered * lax.rsqrt(spread + 1e-05), (1, 0, 2))
+    for i in range(own):
+        mn = (scaled[i] * fgain + fbias).T.astype(BF16)
+        outgoing = jnp.dot(mn, wout_ref[...], preferred_element_type=F32)
+        where = pl.ds(i * tokens, tokens)
+        update_ref[i] = (gate_ref[where] * outgoing + trans_ref[where]).astype(BF16)
+
+
+def fused(mesh, args):
+    pair_repr, chain_ids, valid_counts = args[:3]
+    norm_gain, norm_bias, input_weights, final_gain, final_bias, output_weight, tin, tout = args[3:]
+    rows_n, cols_n = mesh.shape["row"], mesh.shape["col"]
+    peers = rows_n * cols_n
+    tokens = chain_ids.shape[0]
+    own = tokens // peers
+    channels = pair_repr.shape[2]
+    hidden = output_weight.shape[0]
+    share = hidden // peers
+    vmem, anyspace = pl.BlockSpec(memory_space=pltpu.VMEM), pl.BlockSpec(memory_space=pl.ANY)
+    dma = pltpu.SemaphoreType.DMA
+    return pl.pallas_call(
+        functools.partial(kernel, rows_n, cols_n),
+        out_shape=jax.ShapeDtypeStruct((own, tokens, channels), BF16),
+        in_specs=[
+            anyspace,
+            vmem,
+            pl.BlockSpec(memory_space=pltpu.SMEM),
+            vmem,
+            vmem,
+            anyspace,
+            vmem,
+            vmem,
+            anyspace,
+            anyspace,
+            anyspace,
+        ],
+        out_specs=vmem,
+        scratch_shapes=[
+            pltpu.VMEM((own, tokens, channels), BF16),
+            pltpu.VMEM(input_weights.shape, BF16),
+            pltpu.VMEM(output_weight.shape, BF16),
+            pltpu.VMEM(tin.shape, BF16),
+            pltpu.VMEM(tout.shape, BF16),
+            pltpu.VMEM((own * tokens, channels), BF16),
+            pltpu.VMEM((hidden, 2 * own, tokens), BF16),
+            pltpu.VMEM((peers, share, 2 * own, tokens), BF16),
+            pltpu.VMEM((peers, share // 2, 2 * own, tokens), BF16),
+            pltpu.VMEM((peers, share // 2, 2 * own, tokens), BF16),
+            pltpu.VMEM((own * tokens, channels), F32),
+            pltpu.VMEM((own * tokens, channels), F32),
+            dma((5,)),
+            dma((cols_n,)),
+            dma((cols_n,)),
+            dma((peers,)),
+            dma((peers,)),
+            dma((peers,)),
+            dma((peers,)),
+        ],
+        compiler_params=pltpu.CompilerParams(
+            collective_id=0, has_side_effects=True, vmem_limit_bytes=40 * 1024 * 1024
+        ),
+        cost_estimate=pl.CostEstimate(
+            flops=10**9, bytes_accessed=4 * 10**6, transcendentals=10**6
+        ),
+    )(
+        pair_repr,
+        chain_ids.reshape(1, -1),
+        valid_counts,
+        norm_gain.reshape(1, -1),
+        norm_bias.reshape(1, -1),
+        input_weights,
+        final_gain.reshape(1, -1),
+        final_bias.reshape(1, -1),
+        output_weight,
+        tin,
+        tout,
+    )
+
+
+def fits(mesh, args):
+    peers = mesh.shape["row"] * mesh.shape["col"]
+    tokens, hidden = args[1].shape[0], args[8].shape[0]
+    return (
+        tokens == 8 * peers
+        and tokens % 128 == 0
+        and tokens * tokens <= 128 * 128
+        and hidden % (2 * peers) == 0
+        and args[0].shape[1] % 16 == 0
+        and args[0].shape[2] == 128
+    )
 
 
 def token_valid_of(chain_ids, valid_counts):
@@ -101,4 +396,8 @@
         P(),
     )
     out_specs = P(("group", "row", "col"), None, None)
-    return jax.shard_map(local, mesh=mesh, in_specs=in_specs, out_specs=out_specs, check_vma=False)
+
+    def part(*args):
+        return fused(mesh, args) if fits(mesh, args) else local(*args)
+
+    return jax.shard_map(part, mesh=mesh, in_specs=in_specs, out_specs=out_specs, check_vma=False)

time: 102 us -> 30.8 us (0.30)
  blocking collectives: 32.6 us -> 0 us
  waiting for transfers between devices: 30.2 us -> 0 us
  Pallas kernels: 0 us -> 24.6 us
  between operations: 13.6 us -> 0.03 us
  other arithmetic: 9.34 us -> 0 us
  matrix products: 5.73 us -> 0 us
  local copies, waits for them, and re-layouts: 9.73 us -> 5.83 us
    reduce_scatter x1 -> x0, waiting for transfers between devices: 30.2 us -> none  [local(): lax.psum_scatter(partials, 'col', scatter_dimension=1, tiled=True)]
    pallas_call x0 -> x1, Pallas kernels: none -> 24.6 us  [fused(): pl.pallas_call(functools.partial(kernel, rows_n, cols_n), out_shape=jax.S...]
    all_gather x1 -> x0, blocking collectives: 24.2 us -> none  [local(): lax.all_gather(right_side, 'row', axis=0, tiled=True)]
    all_to_all x1 -> x0, blocking collectives: 8.42 us -> none  [local(): lax.all_to_all(update_tile, 'col', split_axis=0, concat_axis=1, tiled=True)]
    reduce_sum x6 -> x0, other arithmetic: 6.06 us -> none  [the longest x2 2.75 us: layer_norm(): spread = jnp.mean(centered * centered, axis=-1, keepdims=True)]
    dot_general x5 -> x0, matrix products: 5.73 us -> none  [the longest x1 2.85 us: local(): jnp.einsum('ikc,jkc->ijc', left_side, lax.all_gather(right_side, 'row', a...]
    unnamed x14 -> x23, local copies, waits for them, and re-layouts: 0.23 us -> 5.83 us
    all_gather x1 -> x0, local copies, waits for them, and re-layouts: 3.92 us -> none  [local(): lax.all_gather(right_side, 'row', axis=0, tiled=True)]
  transfers between devices with their start and end apart: 1 -> 0, of which waited for: 1 -> 0; matrix products, arithmetic and copies ran while one was open for 1% -> 0% of each run, Pallas kernels for 0% -> 0%
where the time goes in v1:
time: 30.8 us; the launch traced here: 30.5 us
  Pallas kernels  24.6 us (80%)
  local copies, waits for them, and re-layouts  5.83 us (19%)
    pallas_call x1, Pallas kernels, fused(): pl.pallas_call(functools.partial(kernel, rows_n, cols_n), out_shape=jax.S...  24.6 us
    unnamed x23, local copies, waits for them, and re-layouts  5.83 us

profile of v1, /device:TPU:0, one launch (start us, length us, event | category | flops | bytes accessed | tf_op | source)
XLA Modules:
  0.0 30.5 jit_solution(8225089803800020890)
XLA Ops:
  0.0 0.0 copy-start.8
  0.0 0.0 copy-start.9
  0.0 0.0 copy-start.10
  0.0 0.0 copy-start.5
  0.0 0.0 copy-start.6
  0.0 0.0 copy-start.7
  0.0 0.6 %copy-done.8 = f32[128]{0:T(128)S(1)} copy-done((f32[128]{0:T(128)S(1)}, f32[128]{0:T(128)}, u32[]{:S(2)}) %copy-start.8) | copy-done | bytes 536
  0.7 0.0 copy-done.9
  0.7 0.0 copy-done.10
  0.7 0.0 copy-done.5
  0.7 0.0 copy-done.6
  0.7 0.0 copy-done.7
  0.7 0.0 copy-start
  0.7 0.9 %copy-done = bf16[32,32,128]{2,1,0:T(8,128)(2,1)S(1)} copy-done((bf16[32,32,128]{2,1,0:T(8,128)(2,1)S(1)}, bf16[32,32,128]{2,1,0:T(8,128)(2,1)}, u32[]{:S(2)}) %copy-start) | copy-done | bytes 262168
  1.7 0.0 copy-start.1
  1.7 0.9 %copy-done.1 = bf16[128,1024]{1,0:T(8,128)(2,1)S(1)} copy-done((bf16[128,1024]{1,0:T(8,128)(2,1)S(1)}, bf16[128,1024]{1,0:T(8,128)(2,1)}, u32[]{:S(2)}) %copy-start.1) | copy-done | bytes 262168
  2.6 0.0 copy-start.2
  2.6 0.9 %copy-done.2 = bf16[512,128]{1,0:T(8,128)(2,1)S(1)} copy-done((bf16[512,128]{1,0:T(8,128)(2,1)S(1)}, bf16[512,128]{1,0:T(8,128)(2,1)}, u32[]{:S(2)}) %copy-start.2) | copy-done | bytes 131096
  3.5 0.0 copy-start.3
  3.5 0.9 %copy-done.3 = bf16[128,384]{1,0:T(8,128)(2,1)S(1)} copy-done((bf16[128,384]{1,0:T(8,128)(2,1)S(1)}, bf16[128,384]{1,0:T(8,128)(2,1)}, u32[]{:S(2)}) %copy-start.3) | copy-done | bytes 98328
  4.4 0.0 copy-start.4
  4.4 0.7 %copy-done.4 = bf16[64,128]{1,0:T(8,128)(2,1)S(1)} copy-done((bf16[64,128]{1,0:T(8,128)(2,1)S(1)}, bf16[64,128]{1,0:T(8,128)(2,1)}, u32[]{:S(2)}) %copy-start.4) | copy-done | bytes 16408
  5.2 24.6 %shard_map.109 = bf16[8,128,128]{2,1,0:T(8,128)(2,1)S(1)} custom-call(bf16[32,32,128]{2,1,0:T(8,128)(2,1)S(1)} %copy-done, s32[1,128]{1,0:T(1,128)S(1)} %bitcast.5, s32[8]{0:T(128)S(1)} %copy-done.6, f32[1,128]{1,0:T(1,128)S(1)} %bitcast.6, f32[1,128]{1,0:T(1,128)S(1)} %bitcast.7, bf16[128,384]{1,0:T(8,128)(2,1)S(1)} %copy-done.3, f32[1,64]{1,0:T(1,128)S(1)} %bitcast.8, ...), custom_call_target="tpu_custom_call" | custom-call | flops 1000000000 | bytes 4000000 | tf_op jit(solution)/shard_map/pallas_call | solution.py:230
  29.8 0.7 %copy.13 = bf16[8,128,128]{2,1,0:T(8,128)(2,1)} copy(bf16[8,128,128]{2,1,0:T(8,128)(2,1)S(1)} %shard_map.109) | data formatting | bytes 524288
Async XLA Ops:
  0.0 0.7 %copy-start.8 = (f32[128]{0:T(128)S(1)}, f32[128]{0:T(128)}, u32[]{:S(2)}) copy-start(f32[128]{0:T(128)} %param.15) | copy-start | bytes 1540
  0.0 0.7 %copy-start.9 = (f32[64]{0:T(128)S(1)}, f32[64]{0:T(128)}, u32[]{:S(2)}) copy-start(f32[64]{0:T(128)} %param.17) | copy-start | bytes 772
  0.0 0.7 %copy-start.10 = (f32[64]{0:T(128)S(1)}, f32[64]{0:T(128)}, u32[]{:S(2)}) copy-start(f32[64]{0:T(128)} %param.18) | copy-start | bytes 772
  0.0 0.7 %copy-start.5 = (s32[128]{0:T(128)S(1)}, s32[128]{0:T(128)}, u32[]{:S(2)}) copy-start(s32[128]{0:T(128)} %param.12) | copy-start | bytes 1540
  0.0 0.7 %copy-start.6 = (s32[8]{0:T(128)S(1)}, s32[8]{0:T(128)}, u32[]{:S(2)}) copy-start(s32[8]{0:T(128)} %counts_ref.1) | copy-start | bytes 100
  0.0 0.7 %copy-start.7 = (f32[128]{0:T(128)S(1)}, f32[128]{0:T(128)}, u32[]{:S(2)}) copy-start(f32[128]{0:T(128)} %param.14) | copy-start | bytes 1540
  0.7 0.9 %copy-start = (bf16[32,32,128]{2,1,0:T(8,128)(2,1)S(1)}, bf16[32,32,128]{2,1,0:T(8,128)(2,1)}, u32[]{:S(2)}) copy-start(bf16[32,32,128]{2,1,0:T(8,128)(2,1)} %pair_ref.1) | copy-start | bytes 786436
  1.7 0.9 %copy-start.1 = (bf16[128,1024]{1,0:T(8,128)(2,1)S(1)}, bf16[128,1024]{1,0:T(8,128)(2,1)}, u32[]{:S(2)}) copy-start(bf16[128,1024]{1,0:T(8,128)(2,1)} %tin_hbm.1) | copy-start | bytes 786436
  2.6 0.9 %copy-start.2 = (bf16[512,128]{1,0:T(8,128)(2,1)S(1)}, bf16[512,128]{1,0:T(8,128)(2,1)}, u32[]{:S(2)}) copy-start(bf16[512,128]{1,0:T(8,128)(2,1)} %tout_hbm.1) | copy-start | bytes 393220
  3.5 0.9 %copy-start.3 = (bf16[128,384]{1,0:T(8,128)(2,1)S(1)}, bf16[128,384]{1,0:T(8,128)(2,1)}, u32[]{:S(2)}) copy-start(bf16[128,384]{1,0:T(8,128)(2,1)} %in_hbm.1) | copy-start | bytes 294916
  4.4 0.7 %copy-start.4 = (bf16[64,128]{1,0:T(8,128)(2,1)S(1)}, bf16[64,128]{1,0:T(8,128)(2,1)}, u32[]{:S(2)}) copy-start(bf16[64,128]{1,0:T(8,128)(2,1)} %out_hbm.1) | copy-start | bytes 49156

commit v2 on v1

--- a/solution.py
+++ b/solution.py
@@ -25,18 +25,24 @@
     rows_n,
     cols_n,
     pair_ref,
-    ids_ref,
-    counts_ref,
-    gain_ref,
-    bias_ref,
+    ids_hbm,
+    counts_hbm,
+    gain_hbm,
+    bias_hbm,
     in_hbm,
-    fgain_ref,
-    fbias_ref,
+    fgain_hbm,
+    fbias_hbm,
     out_hbm,
     tin_hbm,
     tout_hbm,
     update_ref,
     x_ref,
+    ids_ref,
+    counts_ref,
+    gain_ref,
+    bias_ref,
+    fgain_ref,
+    fbias_ref,
     win_ref,
     wout_ref,
     tin_ref,
@@ -80,7 +86,18 @@
         )
     ]
     for n, (a, b) in enumerate(
-        ((in_hbm, win_ref), (out_hbm, wout_ref), (tin_hbm, tin_ref), (tout_hbm, tout_ref))
+        (
+            (ids_hbm, ids_ref),
+            (counts_hbm, counts_ref),
+            (gain_hbm, gain_ref),
+            (bias_hbm, bias_ref),
+            (fgain_hbm, fgain_ref),
+            (fbias_hbm, fbias_ref),
+            (in_hbm, win_ref),
+            (out_hbm, wout_ref),
+            (tin_hbm, tin_ref),
+            (tout_hbm, tout_ref),
+        )
     ):
         locals_.append(pltpu.make_async_copy(a, b, local_sem.at[n + 1]))
     for c in locals_:
@@ -103,13 +120,16 @@
     for c in copies:
         c.start()
 
+    for c in locals_:
+        c.wait()
+    counts = counts_ref[...]
     ids = ids_ref[...]
     first = jnp.zeros(ids.shape, F32)
     limit = jnp.zeros(ids.shape, jnp.int32)
-    for label in range(counts_ref.shape[0]):
+    for label in range(counts.shape[1]):
         start = jnp.sum(jnp.where(ids < label, 1.0, 0.0), axis=1, keepdims=True)
         first = jnp.where(ids == label, start, first)
-        limit = jnp.where(ids == label, counts_ref[label], limit)
+        limit = jnp.where(ids == label, counts[:, label : label + 1], limit)
     spot = lax.broadcasted_iota(jnp.int32, ids.shape, 1).astype(F32)
     valid = jnp.where(spot - first < limit.astype(F32), 1.0, 0.0)
     wide = (own, tokens)
@@ -119,8 +139,6 @@
     valid_rows = jnp.sum(jnp.where(mine, valid, 0.0), axis=1, keepdims=True)
     pair_valid = valid_rows * valid
     fgain, fbias = column_of(fgain_ref[...]), column_of(fbias_ref[...])
-    for c in locals_:
-        c.wait()
     in_t = win_ref[:, : 4 * hidden].astype(F32).T.astype(BF16)
     for c in copies:
         c.wait()
@@ -225,27 +243,21 @@
     channels = pair_repr.shape[2]
     hidden = output_weight.shape[0]
     share = hidden // peers
-    vmem, anyspace = pl.BlockSpec(memory_space=pltpu.VMEM), pl.BlockSpec(memory_space=pl.ANY)
+    vmem, hbm = pl.BlockSpec(memory_space=pltpu.VMEM), pl.BlockSpec(memory_space=pltpu.HBM)
     dma = pltpu.SemaphoreType.DMA
     return pl.pallas_call(
         functools.partial(kernel, rows_n, cols_n),
         out_shape=jax.ShapeDtypeStruct((own, tokens, channels), BF16),
-        in_specs=[
-            anyspace,
-            vmem,
-            pl.BlockSpec(memory_space=pltpu.SMEM),
-            vmem,
-            vmem,
-            anyspace,
-            vmem,
-            vmem,
-            anyspace,
-            anyspace,
-            anyspace,
-        ],
+        in_specs=[hbm] * 11,
         out_specs=vmem,
         scratch_shapes=[
             pltpu.VMEM((own, tokens, channels), BF16),
+            pltpu.VMEM((1, tokens), jnp.int32),
+            pltpu.VMEM((1, valid_counts.shape[0]), jnp.int32),
+            pltpu.VMEM((1, channels), F32),
+            pltpu.VMEM((1, channels), F32),
+            pltpu.VMEM((1, hidden), F32),
+            pltpu.VMEM((1, hidden), F32),
             pltpu.VMEM(input_weights.shape, BF16),
             pltpu.VMEM(output_weight.shape, BF16),
             pltpu.VMEM(tin.shape, BF16),
@@ -257,7 +269,7 @@
             pltpu.VMEM((peers, share // 2, 2 * own, tokens), BF16),
             pltpu.VMEM((own * tokens, channels), F32),
             pltpu.VMEM((own * tokens, channels), F32),
-            dma((5,)),
+            dma((11,)),
             dma((cols_n,)),
             dma((cols_n,)),
             dma((peers,)),
@@ -266,7 +278,7 @@
             dma((peers,)),
         ],
         compiler_params=pltpu.CompilerParams(
-            collective_id=0, has_side_effects=True, vmem_limit_bytes=40 * 1024 * 1024
+            collective_id=0, has_side_effects=True, vmem_limit_bytes=65000000
         ),
         cost_estimate=pl.CostEstimate(
             flops=10**9, bytes_accessed=4 * 10**6, transcendentals=10**6
@@ -274,7 +286,7 @@
     )(
         pair_repr,
         chain_ids.reshape(1, -1),
-        valid_counts,
+        valid_counts.reshape(1, -1),
         norm_gain.reshape(1, -1),
         norm_bias.reshape(1, -1),
         input_weights,

time: 30.8 us -> 26.7 us (0.87)
  local copies, waits for them, and re-layouts: 5.83 us -> 1.67 us
    unnamed x23 -> x1, local copies, waits for them, and re-layouts: 5.83 us -> 1.67 us
where the time goes in v2:
time: 26.7 us; the launch traced here: 26.6 us
  Pallas kernels  24.9 us (93%)
  local copies, waits for them, and re-layouts  1.67 us (6%)
    pallas_call x1, Pallas kernels, fused(): pl.pallas_call(functools.partial(kernel, rows_n, cols_n), out_shape=jax.S...  24.9 us
    unnamed x1, local copies, waits for them, and re-layouts  1.67 us

profile of v2, /device:TPU:0, one launch (start us, length us, event | category | flops | bytes accessed | tf_op | source)
XLA Modules:
  0.0 26.6 jit_solution(15903668535166281259)
XLA Ops:
  0.0 24.9 %shard_map.109 = bf16[8,128,128]{2,1,0:T(8,128)(2,1)} custom-call(bf16[32,32,128]{2,1,0:T(8,128)(2,1)} %pair_ref.1, s32[1,128]{1,0:T(1,128)} %bitcast.6, s32[1,8]{1,0:T(1,128)} %bitcast.7, f32[1,128]{1,0:T(1,128)} %bitcast.8, f32[1,128]{1,0:T(1,128)} %bitcast.9, bf16[128,384]{1,0:T(8,128)(2,1)} %in_hbm.1, f32[1,64]{1,0:T(1,128)} %bitcast.10, ...), custom_call_target="tpu_custom_call" | custom-call | flops 1000000000 | bytes 4000000 | tf_op jit(solution)/shard_map/pallas_call | solution.py:248
  24.9 1.7 %copy.13 = bf16[8,128,128]{2,1,0:T(8,128)(2,1)} copy(bf16[8,128,128]{2,1,0:T(8,128)(2,1)} %shard_map.109) | data formatting | bytes 524288

commit v3 on v2

--- a/solution.py
+++ b/solution.py
@@ -37,6 +37,7 @@
     tout_hbm,
     update_ref,
     x_ref,
+    block_ref,
     ids_ref,
     counts_ref,
     gain_ref,
@@ -87,6 +88,7 @@
     ]
     for n, (a, b) in enumerate(
         (
+            (pair_ref, block_ref),
             (ids_hbm, ids_ref),
             (counts_hbm, counts_ref),
             (gain_hbm, gain_ref),
@@ -102,12 +104,10 @@
         locals_.append(pltpu.make_async_copy(a, b, local_sem.at[n + 1]))
     for c in locals_:
         c.start()
-    pl.semaphore_wait(barrier, peers - 1)
-
-    copies = []
+    exchange = []
     for o in range(1, cols_n):
         to = lax.rem(col + o, cols_n)
-        copies.append(
+        exchange.append(
             pltpu.make_async_remote_copy(
                 src_ref=pair_ref.at[pl.ds(to * own, own)],
                 dst_ref=x_ref.at[:, pl.ds(col * width, width), :],
@@ -117,11 +117,9 @@
                 device_id_type=MESH,
             )
         )
-    for c in copies:
-        c.start()
-
     for c in locals_:
         c.wait()
+
     counts = counts_ref[...]
     ids = ids_ref[...]
     first = jnp.zeros(ids.shape, F32)
@@ -132,25 +130,39 @@
         limit = jnp.where(ids == label, counts[:, label : label + 1], limit)
     spot = lax.broadcasted_iota(jnp.int32, ids.shape, 1).astype(F32)
     valid = jnp.where(spot - first < limit.astype(F32), 1.0, 0.0)
-    wide = (own, tokens)
-    mine = lax.broadcasted_iota(jnp.int32, wide, 1) == (
-        me * own + lax.broadcasted_iota(jnp.int32, wide, 0)
-    )
-    valid_rows = jnp.sum(jnp.where(mine, valid, 0.0), axis=1, keepdims=True)
-    pair_valid = valid_rows * valid
-    fgain, fbias = column_of(fgain_ref[...]), column_of(fbias_ref[...])
+    wide, square = (own, tokens), (tokens, tokens)
+    token = lax.broadcasted_iota(jnp.int32, wide, 1)
+    in_row = (
+        (token // (own * cols_n) == row)
+        & (token % own == lax.broadcasted_iota(jnp.int32, wide, 0))
+    )
+    token = lax.broadcasted_iota(jnp.int32, square, 0)
+    lane = lax.broadcasted_iota(jnp.int32, square, 1)
+    to_row = ((token // own) % cols_n == lane // width).astype(F32).astype(BF16)
+    to_token = (token == col * width + lane % width).astype(F32).astype(BF16)
+    valid_rows = jnp.dot(
+        jnp.where(in_row, valid, 0.0).astype(BF16), to_row, preferred_element_type=F32
+    )
+    valid_tokens = jnp.dot(
+        jnp.broadcast_to(valid, wide).astype(BF16), to_token, preferred_element_type=F32
+    )
+    pair_valid = valid_rows * valid_tokens
+
+    gain, bias = gain_ref[...], bias_ref[...]
+
+    def norm(values):
+        values = values.astype(F32)
+        average = jnp.mean(values, axis=-1, keepdims=True)
+        centered = values - average
+        spread = jnp.mean(centered * centered, axis=-1, keepdims=True)
+        return (centered * lax.rsqrt(spread + 1e-05) * gain + bias).astype(BF16)
+
     in_t = win_ref[:, : 4 * hidden].astype(F32).T.astype(BF16)
-    for c in copies:
-        c.wait()
-
-    x = x_ref[...].reshape(own * tokens, channels).astype(F32)
-    average = jnp.mean(x, axis=-1, keepdims=True)
-    centered = x - average
-    spread = jnp.mean(centered * centered, axis=-1, keepdims=True)
-    normed = (centered * lax.rsqrt(spread + 1e-05) * gain_ref[...] + bias_ref[...]).astype(BF16)
-    normed_ref[...] = normed
-
-    projected = lax.dot_general(in_t, normed, (((1,), (1,)), ((), ())), preferred_element_type=F32)
+    block = block_ref[...].reshape(cols_n, own, width, channels)
+    block = jnp.transpose(block, (1, 0, 2, 3)).reshape(own * tokens, channels)
+    projected = lax.dot_general(
+        in_t, norm(block), (((1,), (1,)), ((), ())), preferred_element_type=F32
+    )
     left = sigmoid(projected[hidden : 2 * hidden]) * projected[:hidden]
     right = sigmoid(projected[3 * hidden :]) * projected[2 * hidden : 3 * hidden]
 
@@ -160,24 +172,71 @@
 
     both = jnp.concatenate([by_channel(left), by_channel(right)], axis=1)
     lr_ref[...] = both.astype(BF16)
-
+    fgain, fbias = column_of(fgain_ref[...]), column_of(fbias_ref[...])
+
+    pl.semaphore_wait(barrier, peers - 1)
+    groups = share // 2
     sends = []
-    for o in range(1, peers):
-        device, peer = at(o)
-        sends.append(
-            pltpu.make_async_remote_copy(
-                src_ref=lr_ref.at[pl.ds(peer * share, share)],
-                dst_ref=rx_ref.at[me],
-                send_sem=a_send.at[o],
-                recv_sem=a_recv.at[o],
+    for g in range(groups):
+        sends.append([])
+        for o in range(1, peers):
+            device, peer = at(o)
+            copy = pltpu.make_async_remote_copy(
+                src_ref=lr_ref.at[pl.ds(peer * share + 2 * g, 2)],
+                dst_ref=rx_ref.at[g, me],
+                send_sem=a_send.at[g, o],
+                recv_sem=a_recv.at[g, o],
                 device_id=device,
                 device_id_type=MESH,
             )
-        )
-    for c in sends:
+            copy.start()
+            sends[g].append(copy)
+    for c in exchange:
         c.start()
-    rx_ref[me] = lr_ref[pl.ds(me * share, share)]
-
+    for g in range(groups):
+        rx_ref[g, me] = lr_ref[pl.ds(me * share + 2 * g, 2)]
+
+    backs = []
+    for g in range(groups):
+        for c in sends[g]:
+            c.wait_recv()
+        got = rx_ref[g].astype(F32).reshape(rows_n, cols_n, 2 * 2 * own, tokens)
+        lane = lax.broadcasted_iota(jnp.int32, (1, 1, tokens), 2) // width
+        full = []
+        for a in range(cols_n):
+            rows = got[:, a]
+            for c in range(cols_n):
+                if c != a:
+                    moved = pltpu.roll(
+                        got[:, c].reshape(-1, tokens), ((c - a) % cols_n) * width, 1
+                    ).reshape(rows.shape)
+                    rows = jnp.where(lane == c, moved, rows)
+            full.append(rows.reshape(rows_n, 2, 2, own, tokens))
+        full = jnp.stack(full, axis=1)
+        mixed = []
+        for h in range(2):
+            lh = full[:, :, h, 0].reshape(tokens, tokens).astype(BF16)
+            rh = full[:, :, h, 1].reshape(tokens, tokens).astype(BF16)
+            m = lax.dot_general(lh, rh, (((1,), (1,)), ((), ())), preferred_element_type=F32)
+            mixed.append(m.reshape(peers, own, tokens))
+        tx_ref[g] = jnp.concatenate(mixed, axis=1).astype(BF16)
+        for o in range(1, peers):
+            device, peer = at(o)
+            copy = pltpu.make_async_remote_copy(
+                src_ref=tx_ref.at[g, peer],
+                dst_ref=mx_ref.at[me, g],
+                send_sem=b_send.at[g, o],
+                recv_sem=b_recv.at[g, o],
+                device_id=device,
+                device_id_type=MESH,
+            )
+            copy.start()
+            backs.append(copy)
+        mx_ref[me, g] = tx_ref[g, me]
+
+    for c in exchange:
+        c.wait()
+    normed_ref[...] = norm(x_ref[...].reshape(own * tokens, channels))
     gate_ref[...] = sigmoid(
         jnp.dot(normed_ref[...], win_ref[:, 4 * hidden :], preferred_element_type=F32)
     )
@@ -191,33 +250,9 @@
         act = (ta * sigmoid(ta) * tb).astype(BF16)
         trans_ref[where] = jnp.dot(act, tout_ref[...], preferred_element_type=F32)
 
-    for c in sends:
-        c.wait()
-    mixed = []
-    for h in range(share):
-        block = rx_ref[:, h].astype(F32)
-        lh = block[:, :own].reshape(tokens, tokens).astype(BF16)
-        rh = block[:, own:].reshape(tokens, tokens).astype(BF16)
-        m = lax.dot_general(lh, rh, (((1,), (1,)), ((), ())), preferred_element_type=F32)
-        mixed.append(m.reshape(peers, own, tokens))
-    for n in range(share // 2):
-        tx_ref[:, n] = jnp.concatenate(mixed[2 * n : 2 * n + 2], axis=1).astype(BF16)
-    backs = []
-    for o in range(1, peers):
-        device, peer = at(o)
-        backs.append(
-            pltpu.make_async_remote_copy(
-                src_ref=tx_ref.at[peer],
-                dst_ref=mx_ref.at[me],
-                send_sem=b_send.at[o],
-                recv_sem=b_recv.at[o],
-                device_id=device,
-                device_id_type=MESH,
-            )
-        )
-    for c in backs:
-        c.start()
-    mx_ref[me] = tx_ref[me]
+    for g in range(groups):
+        for c in sends[g]:
+            c.wait_send()
     for c in backs:
         c.wait()
 
@@ -252,6 +287,7 @@
         out_specs=vmem,
         scratch_shapes=[
             pltpu.VMEM((own, tokens, channels), BF16),
+            pltpu.VMEM(pair_repr.shape, BF16),
             pltpu.VMEM((1, tokens), jnp.int32),
             pltpu.VMEM((1, valid_counts.shape[0]), jnp.int32),
             pltpu.VMEM((1, channels), F32),
@@ -264,18 +300,18 @@
             pltpu.VMEM(tout.shape, BF16),
             pltpu.VMEM((own * tokens, channels), BF16),
             pltpu.VMEM((hidden, 2 * own, tokens), BF16),
-            pltpu.VMEM((peers, share, 2 * own, tokens), BF16),
-            pltpu.VMEM((peers, share // 2, 2 * own, tokens), BF16),
+            pltpu.VMEM((share // 2, peers, 2, 2 * own, tokens), BF16),
+            pltpu.VMEM((share // 2, peers, 2 * own, tokens), BF16),
             pltpu.VMEM((peers, share // 2, 2 * own, tokens), BF16),
             pltpu.VMEM((own * tokens, channels), F32),
             pltpu.VMEM((own * tokens, channels), F32),
-            dma((11,)),
+            dma((12,)),
             dma((cols_n,)),
             dma((cols_n,)),
-            dma((peers,)),
-            dma((peers,)),
-            dma((peers,)),
-            dma((peers,)),
+            dma((share // 2, peers)),
+            dma((share // 2, peers)),
+            dma((share // 2, peers)),
+            dma((share // 2, peers)),
         ],
         compiler_params=pltpu.CompilerParams(
             collective_id=0, has_side_effects=True, vmem_limit_bytes=65000000
@@ -306,8 +342,8 @@
         and tokens % 128 == 0
         and tokens * tokens <= 128 * 128
         and hidden % (2 * peers) == 0
+        and args[0].shape == (8 * mesh.shape["col"], tokens // mesh.shape["col"], 128)
         and args[0].shape[1] % 16 == 0
-        and args[0].shape[2] == 128
     )
 
 

time: 26.7 us -> 23 us (0.86)
  Pallas kernels: 24.9 us -> 21.1 us
    pallas_call x1, Pallas kernels: 24.9 us -> 21.1 us  [fused(): pl.pallas_call(functools.partial(kernel, rows_n, cols_n), out_shape=jax.S...]
where the time goes in v3:
time: 23 us; the launch traced here: 22.8 us
  Pallas kernels  21.1 us (92%)
  local copies, waits for them, and re-layouts  1.67 us (7%)
    pallas_call x1, Pallas kernels, fused(): pl.pallas_call(functools.partial(kernel, rows_n, cols_n), out_shape=jax.S...  21.1 us
    unnamed x1, local copies, waits for them, and re-layouts  1.67 us

profile of v3, /device:TPU:0, one launch (start us, length us, event | category | flops | bytes accessed | tf_op | source)
XLA Modules:
  0.0 22.8 jit_solution(8272308384707426070)
XLA Ops:
  0.0 21.1 %shard_map.109 = bf16[8,128,128]{2,1,0:T(8,128)(2,1)} custom-call(bf16[32,32,128]{2,1,0:T(8,128)(2,1)} %pair_ref.1, s32[1,128]{1,0:T(1,128)} %bitcast.6, s32[1,8]{1,0:T(1,128)} %bitcast.7, f32[1,128]{1,0:T(1,128)} %bitcast.8, f32[1,128]{1,0:T(1,128)} %bitcast.9, bf16[128,384]{1,0:T(8,128)(2,1)} %in_hbm.1, f32[1,64]{1,0:T(1,128)} %bitcast.10, ...), custom_call_target="tpu_custom_call" | custom-call | flops 1000000000 | bytes 4000000 | tf_op jit(solution)/shard_map/pallas_call | solution.py:283
  21.1 1.7 %copy.13 = bf16[8,128,128]{2,1,0:T(8,128)(2,1)} copy(bf16[8,128,128]{2,1,0:T(8,128)(2,1)} %shard_map.109) | data formatting | bytes 524288

commit v4 on v3

--- a/solution.py
+++ b/solution.py
@@ -35,7 +35,7 @@
     out_hbm,
     tin_hbm,
     tout_hbm,
-    update_ref,
+    update_hbm,
     x_ref,
     block_ref,
     ids_ref,
@@ -48,7 +48,6 @@
     wout_ref,
     tin_ref,
     tout_ref,
-    normed_ref,
     lr_ref,
     rx_ref,
     tx_ref,
@@ -56,6 +55,7 @@
     gate_ref,
     trans_ref,
     local_sem,
+    out_sem,
     in_send,
     in_recv,
     a_send,
@@ -104,9 +104,10 @@
         locals_.append(pltpu.make_async_copy(a, b, local_sem.at[n + 1]))
     for c in locals_:
         c.start()
+    partners = (col + 1 - 2 * lax.rem(col, 2), lax.rem(col + 2, 4), 3 - col)
     exchange = []
     for o in range(1, cols_n):
-        to = lax.rem(col + o, cols_n)
+        to = partners[o - 1]
         exchange.append(
             pltpu.make_async_remote_copy(
                 src_ref=pair_ref.at[pl.ds(to * own, own)],
@@ -175,6 +176,8 @@
     fgain, fbias = column_of(fgain_ref[...]), column_of(fbias_ref[...])
 
     pl.semaphore_wait(barrier, peers - 1)
+    for c in exchange:
+        c.start()
     groups = share // 2
     sends = []
     for g in range(groups):
@@ -191,13 +194,32 @@
             )
             copy.start()
             sends[g].append(copy)
-    for c in exchange:
-        c.start()
     for g in range(groups):
         rx_ref[g, me] = lr_ref[pl.ds(me * share + 2 * g, 2)]
 
+    def own_rows(source):
+        where = pl.ds(pl.multiple_of(source * width, width), width)
+        flat, whole = (own * width, channels), (own, width, channels)
+        normed = norm(x_ref[:, where, :].reshape(flat))
+        gate = sigmoid(jnp.dot(normed, win_ref[:, 4 * hidden :], preferred_element_type=F32))
+        gate_ref[:, where, :] = gate.reshape(whole)
+        part = jnp.dot(normed, tin_ref[...], preferred_element_type=F32)
+        ta, tb = part[:, :trans], part[:, trans:]
+        act = (ta * sigmoid(ta) * tb).astype(BF16)
+        out = jnp.dot(act, tout_ref[...], preferred_element_type=F32)
+        trans_ref[:, where, :] = out.reshape(whole)
+
+    def rest(offsets):
+        for o in offsets:
+            exchange[o - 1].wait_recv()
+            own_rows(partners[o - 1])
+
+    own_rows(col)
+    rest((1,))
     backs = []
     for g in range(groups):
+        if g == 1:
+            rest(())
         for c in sends[g]:
             c.wait_recv()
         got = rx_ref[g].astype(F32).reshape(rows_n, cols_n, 2 * 2 * own, tokens)
@@ -234,25 +256,12 @@
             backs.append(copy)
         mx_ref[me, g] = tx_ref[g, me]
 
-    for c in exchange:
-        c.wait()
-    normed_ref[...] = norm(x_ref[...].reshape(own * tokens, channels))
-    gate_ref[...] = sigmoid(
-        jnp.dot(normed_ref[...], win_ref[:, 4 * hidden :], preferred_element_type=F32)
-    )
-    step = 128
-
-    @pl.loop(0, own * tokens // step)
-    def _(n):
-        where = pl.ds(pl.multiple_of(n * step, step), step)
-        part = jnp.dot(normed_ref[where], tin_ref[...], preferred_element_type=F32)
-        ta, tb = part[:, :trans], part[:, trans:]
-        act = (ta * sigmoid(ta) * tb).astype(BF16)
-        trans_ref[where] = jnp.dot(act, tout_ref[...], preferred_element_type=F32)
-
+    rest((2, 3))
     for g in range(groups):
         for c in sends[g]:
             c.wait_send()
+    for c in exchange:
+        c.wait_send()
     for c in backs:
         c.wait()
 
@@ -261,11 +270,16 @@
     centered = m - average
     spread = jnp.mean(centered * centered, axis=0, keepdims=True)
     scaled = jnp.transpose(centered * lax.rsqrt(spread + 1e-05), (1, 0, 2))
+    outs = []
     for i in range(own):
         mn = (scaled[i] * fgain + fbias).T.astype(BF16)
         outgoing = jnp.dot(mn, wout_ref[...], preferred_element_type=F32)
-        where = pl.ds(i * tokens, tokens)
-        update_ref[i] = (gate_ref[where] * outgoing + trans_ref[where]).astype(BF16)
+        x_ref[i] = (gate_ref[i] * outgoing + trans_ref[i]).astype(BF16)
+        out = pltpu.make_async_copy(x_ref.at[i], update_hbm.at[i], out_sem.at[i])
+        out.start()
+        outs.append(out)
+    for c in outs:
+        c.wait()
 
 
 def fused(mesh, args):
@@ -284,7 +298,7 @@
         functools.partial(kernel, rows_n, cols_n),
         out_shape=jax.ShapeDtypeStruct((own, tokens, channels), BF16),
         in_specs=[hbm] * 11,
-        out_specs=vmem,
+        out_specs=hbm,
         scratch_shapes=[
             pltpu.VMEM((own, tokens, channels), BF16),
             pltpu.VMEM(pair_repr.shape, BF16),
@@ -298,14 +312,14 @@
             pltpu.VMEM(output_weight.shape, BF16),
             pltpu.VMEM(tin.shape, BF16),
             pltpu.VMEM(tout.shape, BF16),
-            pltpu.VMEM((own * tokens, channels), BF16),
             pltpu.VMEM((hidden, 2 * own, tokens), BF16),
             pltpu.VMEM((share // 2, peers, 2, 2 * own, tokens), BF16),
             pltpu.VMEM((share // 2, peers, 2 * own, tokens), BF16),
             pltpu.VMEM((peers, share // 2, 2 * own, tokens), BF16),
-            pltpu.VMEM((own * tokens, channels), F32),
-            pltpu.VMEM((own * tokens, channels), F32),
+            pltpu.VMEM((own, tokens, channels), F32),
+            pltpu.VMEM((own, tokens, channels), F32),
             dma((12,)),
+            dma((own,)),
             dma((cols_n,)),
             dma((cols_n,)),
             dma((share // 2, peers)),
@@ -340,6 +354,7 @@
     return (
         tokens == 8 * peers
         and tokens % 128 == 0
+        and mesh.shape["col"] == 4
         and tokens * tokens <= 128 * 128
         and hidden % (2 * peers) == 0
         and args[0].shape == (8 * mesh.shape["col"], tokens // mesh.shape["col"], 128)

time: 23 us -> 22.6 us (0.983)
  Pallas kernels: 21.1 us -> 20.7 us
    pallas_call x1, Pallas kernels: 21.1 us -> 20.7 us  [fused(): pl.pallas_call(functools.partial(kernel, rows_n, cols_n), out_shape=jax.S...]
where the time goes in v4:
time: 22.6 us; the launch traced here: 22.4 us
  Pallas kernels  20.7 us (92%)
  local copies, waits for them, and re-layouts  1.67 us (7%)
    pallas_call x1, Pallas kernels, fused(): pl.pallas_call(functools.partial(kernel, rows_n, cols_n), out_shape=jax.S...  20.7 us
    unnamed x1, local copies, waits for them, and re-layouts  1.67 us

profile of v4, /device:TPU:0, one launch (start us, length us, event | category | flops | bytes accessed | tf_op | source)
XLA Modules:
  0.0 22.4 jit_solution(10214366453472134968)
XLA Ops:
  0.0 20.7 %shard_map.109 = bf16[8,128,128]{2,1,0:T(8,128)(2,1)} custom-call(bf16[32,32,128]{2,1,0:T(8,128)(2,1)} %pair_ref.1, s32[1,128]{1,0:T(1,128)} %bitcast.6, s32[1,8]{1,0:T(1,128)} %bitcast.7, f32[1,128]{1,0:T(1,128)} %bitcast.8, f32[1,128]{1,0:T(1,128)} %bitcast.9, bf16[128,384]{1,0:T(8,128)(2,1)} %in_hbm.1, f32[1,64]{1,0:T(1,128)} %bitcast.10, ...), custom_call_target="tpu_custom_call" | custom-call | flops 1000000000 | bytes 4000000 | tf_op jit(solution)/shard_map/pallas_call | solution.py:297
  20.8 1.7 %copy.13 = bf16[8,128,128]{2,1,0:T(8,128)(2,1)} copy(bf16[8,128,128]{2,1,0:T(8,128)(2,1)} %shard_map.109) | data formatting | bytes 524288
